TPU v7x, 256 devices: a whole 4x4x8 slice. The times are simulated.
256 devices in a mesh: band: 16 (over z, core), comp: 16 (over y, x).
Axes of the slice: x: 4, y: 4, z: 8, core: 2. Of those that a mesh axis runs over, the one named last changes fastest.
Arguments:
- spectrum: float32 [1728, 64, 1440], P('comp', 'band'), may hold values from 0.05 to 2
- group_courant: float32 [48], replicated, may hold values from 0.05 to 0.5
- coupling: bfloat16 [1728, 1728], P('band'), may hold values from -0.15625 to 0.15625
- wind_dir: int32 [64, 1440], P('band'), may hold values from 0 to 35
- sea_mask: int32 [64, 1440], P('band'), may hold values from 0 to 1, as said below
- owner_cells: int32 [256, 270], P(('band', 'comp')), may hold values from 0 to 5759, as said below
- owner_counts: int32 [256], P(('band', 'comp')), may hold values from 135 to 270, as said below
Outputs:
- evolved: float32 [1728, 64, 1440], P('comp', 'band')
Inputs may be any that keep to these rules, and one draw needn't show every extreme that they name: `sea_mask`: the land of each band is one run of columns around a centre, widening by row order of a random tie-break; one band has exactly 4320 sea cells, every band at least half of that. `owner_cells`: row b * 16 + c lists the sea cells owned by owner c of band b as row within the band * 1440 + longitude. The first owner_counts entries are the owner's cells in increasing order, the owners of a band take consecutive runs of the band's sea cells in order, every sea cell is listed exactly once, and the remaining entries are 0. `owner_counts`: the counts of the owners of one band differ by at most one and sum to the band's sea cells.
All inputs are finite; a program needn't handle non-finite values.
Results may differ from a plain program's by a relative error of at most 0.0014.
Values may be sent and summed in bfloat16 or wider, within the bound.
A program may use at most 192 MiB of HBM per device.

v0:
```python
import math

import jax
import jax.numpy as jnp
from jax import lax
from jax.sharding import PartitionSpec as P

DIRS = 36
FREQS = 48
SUBSTEPS = 3


first_lat = 30.0
step_time = 0.5
wind_gain = 0.6
damping = 0.4


def padded_2(cells, sides, width):
    for axis, dim in sides:
        count = lax.axis_size(axis)
        ends = count - 1
        head = lax.slice_in_dim(cells, 0, width, axis=dim)
        tail = lax.slice_in_dim(cells, cells.shape[dim] - width, cells.shape[dim], axis=dim)
        cells = jnp.concatenate(
            [
                lax.ppermute(tail, axis, [(i, (i + 1) % count) for i in range(ends)]),
                cells,
                lax.ppermute(head, axis, [((i + 1) % count, i) for i in range(ends)]),
            ],
            axis=dim,
        )
    return cells


def courant_rows(group_courant, comp_index, row_index):
    freq = comp_index % FREQS
    dirn = comp_index // FREQS
    picker = (freq[:, None] == jnp.arange(FREQS, dtype=jnp.int32)[None, :]).astype(jnp.float32)
    speed = jnp.sum(picker * group_courant[None, :], axis=1)
    theta = 2.0 * math.pi / DIRS * dirn.astype(jnp.float32)
    latitude = (first_lat + 0.25 * (row_index.astype(jnp.float32) + 0.5)) * (math.pi / 180.0)
    cross_x = (speed * jnp.cos(theta))[:, None, None] / jnp.cos(latitude)[None, :, None]
    cross_y = (speed * jnp.sin(theta))[:, None, None]
    return (cross_x, cross_y)


def advect(field, south, north, sea, cross_x, cross_y):
    west = jnp.roll(field, 1, axis=2)
    east = jnp.roll(field, -1, axis=2)
    moved = (
        field
        - jnp.maximum(cross_x, 0.0) * (field - west)
        - jnp.minimum(cross_x, 0.0) * (east - field)
    )
    moved = (
        moved
        - jnp.maximum(cross_y, 0.0) * (field - south)
        - jnp.minimum(cross_y, 0.0) * (north - field)
    )
    return moved * sea


def sources(owned, wind_index, transfer):
    comps = owned.shape[0]
    dirn = jnp.arange(comps, dtype=jnp.int32) // FREQS
    angle = 2.0 * math.pi / DIRS * (dirn[:, None] - wind_index[None, :]).astype(jnp.float32)
    facing = jnp.maximum(jnp.cos(angle), 0.0)
    energy = jnp.sum(owned, axis=0) / comps
    growth = wind_gain * facing * owned - damping * energy[None, :] * owned + transfer
    return jnp.maximum(owned + step_time * growth, 0.0)


def body(spectrum, group_courant, coupling, wind_dir, sea_mask, owner_cells, owner_counts):
    kdev, rows, lon = spectrum.shape
    ndevs = lax.axis_size("comp")
    comps = kdev * ndevs
    cells = rows * lon
    capacity = owner_cells.shape[1]
    comp_index = lax.axis_index("comp") * kdev + jnp.arange(kdev, dtype=jnp.int32)
    row_start = lax.axis_index("band") * rows
    sea = sea_mask.astype(jnp.float32)[None]
    cross_x, cross_y = courant_rows(
        group_courant, comp_index, row_start + jnp.arange(rows, dtype=jnp.int32)
    )
    field = spectrum
    for step in range(SUBSTEPS):
        padded = padded_2(field, (("band", 1),), 1)
        field = advect(field, padded[:, :-2], padded[:, 2:], sea, cross_x, cross_y)
    flat = field.reshape(kdev, cells)
    lists, counts = (
        lax.all_gather(owner_cells, "comp", axis=0, tiled=True),
        lax.all_gather(owner_counts, "comp", axis=0, tiled=True),
    )
    wind_own = jnp.take(wind_dir.reshape(-1), owner_cells[0])
    alive = jnp.arange(capacity, dtype=jnp.int32)[None, :] < counts[:, None]
    target = jnp.where(alive, lists, cells)
    outgoing = jnp.take(flat, lists.reshape(-1), axis=1).reshape(kdev, ndevs, capacity)
    owned = lax.all_to_all(outgoing, "comp", split_axis=1, concat_axis=0, tiled=True).reshape(
        comps, capacity
    )
    squared = (owned * owned).astype(jnp.bfloat16)
    transfer = jnp.dot(
        lax.all_gather(coupling, "band", axis=0, tiled=True),
        squared,
        preferred_element_type=jnp.float32,
    )
    updated = sources(owned, wind_own, transfer)
    values = lax.all_to_all(
        updated.reshape(comps, 1, capacity), "comp", split_axis=0, concat_axis=1, tiled=True
    )
    evolved = (
        jnp.zeros((kdev, cells), jnp.float32)
        .at[:, target.reshape(-1)]
        .set(values.reshape(kdev, ndevs * capacity), mode="drop")
    )
    return evolved.reshape(kdev, rows, lon)


def solution(mesh):
    return jax.shard_map(
        body,
        mesh=mesh,
        in_specs=(
            P("comp", "band", None),
            P(),
            P("band", None),
            P("band", None),
            P("band", None),
            P(("band", "comp"), None),
            P(("band", "comp")),
        ),
        out_specs=P("comp", "band", None),
        check_vma=False,
    )
```

profile of v0, /device:TPU:34, one launch (start us, length us, event | category | flops | bytes accessed | tf_op | source)
XLA Modules:
  0.0 269.9 jit_solution(3845505281255447607)
XLA Ops:
  7.3 2.6 copy.38
  10.8 1.9 collective-permute-start
  12.8 3.6 %collective-permute-start.1 = (f32[108,1,1440]{2,0,1:T(8,128)S(1)}, f32[108,1,1440]{2,0,1:T(8,128)}, u32[]{:S(2)}, u32[]{:S(2)}) collective-permute-start(f32[108,1,1440]{2,0,1:T(8,128)S(1)} %get-tuple-element.22), channel_id=1, source_target_pairs={{16,0},{32,16},{48,32},{64,48},{80,64},{96,80},{112,96},{128,112},... | collective-permute-start | bytes 1866248 | tf_op jit(solution)/shard_map/ppermute | solution.py:29
  16.4 23.3 %all-gather = s32[16,1,270]{2,1,0:T(1,128)S(1)} all-gather(s32[1,1,270]{2,1,0:T(1,128)S(1)} %bitcast.51), channel_id=1, replica_groups=mesh['band'=16,'comp'=16] {'comp'}, dimensions={0}, use_global_device_ids=true | all-gather | bytes 18360 | tf_op jit(solution)/shard_map/all_gather | solution.py:92
  41.5 3.8 %fusion.17 = f32[108,4,1440]{2,0,1:T(8,128)S(1)} fusion(f32[108,4,1440]{2,0,1:T(8,128)S(1)} %copy.38, f32[108,1,1440]{2,0,1:T(8,128)} %collective-permute-done.1, f32[108,1,1440]{2,0,1:T(8,128)} %collective-permute-done, f32[108,4,1439]{2,0,1:T(8,128)S(1)} %get-tuple-element.18, f32[108,4,1]{2,0,1:T(8,128)S(1)} %get-tuple-element.20, ...), kind=kLoop, calls=%fused_computation.26 | loop fusion | flops 10575360 | bytes 11224800 | tf_op jit(solution)/shard_map/mul | solution.py:61
  45.4 1.9 collective-permute-start.2
  47.3 3.6 %collective-permute-start.3 = (f32[108,1,1440]{2,0,1:T(8,128)S(1)}, f32[108,1,1440]{2,0,1:T(8,128)S(1)}, u32[]{:S(2)}, u32[]{:S(2)}) collective-permute-start(f32[108,1,1440]{2,0,1:T(8,128)S(1)} %get-tuple-element.16), channel_id=1, source_target_pairs={{16,0},{32,16},{48,32},{64,48},{80,64},{96,80},{112,96},{128,112},... | collective-permute-start | bytes 1866248 | tf_op jit(solution)/shard_map/ppermute | solution.py:29
  52.1 12.0 %collective-permute-done.2 = f32[108,1,1440]{2,0,1:T(8,128)S(1)} collective-permute-done((f32[108,1,1440]{2,0,1:T(8,128)S(1)}, f32[108,1,1440]{2,0,1:T(8,128)S(1)}, u32[]{:S(2)}, u32[]{:S(2)}) %collective-permute-start.2) | collective-permute-done | bytes 622112 | tf_op jit(solution)/shard_map/ppermute | solution.py:27
  64.9 2.7 %fusion.10 = f32[108,4,1440]{2,0,1:T(8,128)S(1)} fusion(f32[108,4,1440]{2,0,1:T(8,128)S(1)} %fusion.17, f32[108,1,1440]{2,0,1:T(8,128)S(1)} %collective-permute-done.3, f32[108,1,1440]{2,0,1:T(8,128)S(1)} %collective-permute-done.2, f32[108,4,1439]{2,0,1:T(8,128)S(1)} %get-tuple-element.12, f32[108,4,1]{2,0,1:T(8,128)S(1)} %get-tuple-element.14, ...), kind=kLoop, calls=%fused_computation.17 | loop fusion | flops 10575360 | bytes 11224800 | tf_op jit(solution)/shard_map/mul | solution.py:61
  67.7 4.1 %collective-permute-start.4 = (f32[108,1,1440]{2,0,1:T(8,128)S(1)}, f32[108,1,1440]{2,0,1:T(8,128)S(1)}, u32[]{:S(2)}, u32[]{:S(2)}) collective-permute-start(f32[108,1,1440]{2,0,1:T(8,128)S(1)} %get-tuple-element.9), channel_id=1, source_target_pairs={{0,16},{16,32},{32,48},{48,64},{64,80},{80,96},{96,112},{112,128},... | collective-permute-start | bytes 1866248 | tf_op jit(solution)/shard_map/ppermute | solution.py:27
  71.8 1.9 collective-permute-start.5
  74.9 5.3 %collective-permute-done.4 = f32[108,1,1440]{2,0,1:T(8,128)S(1)} collective-permute-done((f32[108,1,1440]{2,0,1:T(8,128)S(1)}, f32[108,1,1440]{2,0,1:T(8,128)S(1)}, u32[]{:S(2)}, u32[]{:S(2)}) %collective-permute-start.4) | collective-permute-done | bytes 622112 | tf_op jit(solution)/shard_map/ppermute | solution.py:27
  80.1 2.0 collective-permute-done.5
  82.1 3.8 %fusion.3 = f32[108,4,1440]{2,0,1:T(8,128)} fusion(f32[108,4,1440]{2,0,1:T(8,128)S(1)} %fusion.10, f32[108,1,1440]{2,0,1:T(8,128)S(1)} %collective-permute-done.5, f32[108,1,1440]{2,0,1:T(8,128)S(1)} %collective-permute-done.4, f32[108,4,1439]{2,0,1:T(8,128)S(1)} %get-tuple-element.6, f32[108,4,1]{2,0,1:T(8,128)S(1)} %get-tuple-element.8, ...), kind=kLoop, calls=%fused_computation.8 | loop fusion | flops 10575360 | bytes 11224800 | tf_op jit(solution)/shard_map/mul | solution.py:61
  86.0 2.3 copy.48
  88.3 8.8 %gather_fusion = f32[4320,108]{1,0:T(8,128)} fusion(f32[108,5760]{0,1:T(8,128)S(1)} %bitcast.45, s32[5120]{0:T(1024)S(1)} %pad_clamp_fusion), kind=kCustom, calls=%fused_computation | custom fusion | bytes 3749760 | tf_op jit(solution)/shard_map/jit(_take)/gather | solution.py:98
  98.8 1.7 broadcast_select_fusion
  100.5 7.6 %all-to-all-start = ((f32[108,16,270]{0,2,1:T(8,128)}), f32[108,16,270]{0,2,1:T(8,128)S(1)}, u32[]{:S(2)}, u32[]{:S(2)}) async-start(f32[108,16,270]{0,2,1:T(8,128)} %broadcast_select_fusion), calls=%async_computation | async-start | bytes 4456448 | tf_op jit(solution)/shard_map/all_to_all | solution.py:99
  108.2 2.2 gather_fusion.1
  110.5 28.4 %all-to-all-done = f32[108,16,270]{0,2,1:T(8,128)S(1)} async-done(((f32[108,16,270]{0,2,1:T(8,128)}), f32[108,16,270]{0,2,1:T(8,128)S(1)}, u32[]{:S(2)}, u32[]{:S(2)}) %all-to-all-start) | async-done | bytes 1866272 | tf_op jit(solution)/shard_map/all_to_all | solution.py:99
  138.9 2.0 copy.49
  141.0 3.3 %reshape.266 = f32[1728,270]{0,1:T(8,128)} reshape(f32[16,108,1,270]{1,0,3,2:T(8,128)} %copy.49) | data formatting | bytes 3732480 | tf_op jit(solution)/shard_map/reshape | solution.py:99
  144.5 8.8 %reshape.301 = bf16[1728,1728]{1,0:T(8,128)(2,1)} reshape(bf16[16,108,1728]{2,1,0:T(8,128)(2,1)} %all-gather.4.cloned.1.call-done) | data formatting | bytes 11943936
  153.3 11.7 %fusion.37 = f32[1728,1,270]{0,2,1:T(8,128)S(1)} fusion(f32[1728,270]{0,1:T(8,128)} %reshape.266, bf16[1728,1728]{1,0:T(8,128)(2,1)} %reshape.301, f32[270]{0:T(512)S(1)} %broadcast_multiply_fusion, s32[270]{0:T(512)S(1)} %fusion.47, s32[1728]{0:T(1024)S(1)} %add_select_fusion), kind=kOutput, calls=%fused_computation.53 | convolution fusion | flops 1618963200 | bytes 9713520 | tf_op jit(solution)/shard_map/dot_general | solution.py:103
  165.0 4.9 %copy.50 = f32[1728,1,270]{2,1,0:T(1,128)} copy(f32[1728,1,270]{0,2,1:T(8,128)S(1)} %fusion.37) | data formatting | bytes 3732480 | tf_op jit(solution)/shard_map/reshape | solution.py:110
  169.9 8.6 %all-to-all-start.1 = ((f32[1728,1,270]{2,1,0:T(1,128)}), f32[1728,1,270]{2,1,0:T(1,128)S(1)}, u32[]{:S(2)}, u32[]{:S(2)}) async-start(f32[1728,1,270]{2,1,0:T(1,128)} %copy.50), calls=%async_computation.1 | async-start | bytes 5308416 | tf_op jit(solution)/shard_map/all_to_all | solution.py:109
  180.5 47.6 %all-reduce = s32[16]{0:T(128)S(1)} all-reduce(s32[16]{0:T(128)S(1)} %dynamic-update-slice), channel_id=1, replica_groups=mesh['band'=16,'comp'=16] {'comp'}, use_global_device_ids=true, to_apply=%add | all-reduce | flops 16 | bytes 128
  228.4 5.7 %copy.51 = f32[1728,1,270]{0,2,1:T(8,128)} copy(f32[1728,1,270]{2,1,0:T(1,128)S(1)} %all-to-all-done.1) | data formatting | bytes 3732480 | tf_op jit(solution)/shard_map/all_to_all | solution.py:109
  234.1 4.4 %all_to_all.26 = f32[16,108,1,270]{1,0,3,2:T(8,128)} reshape(f32[1728,1,270]{0,2,1:T(8,128)} %copy.51) | data formatting | bytes 3732480 | tf_op jit(solution)/shard_map/all_to_all | solution.py:109
  238.5 2.3 copy.52
  242.3 17.9 %scatter_custom_fusion = f32[108,5760]{0,1:T(8,128)S(1)} fusion(s32[4320]{0:T(1024)S(1)} %fusion.41, f32[108,4320]{0,1:T(8,128)} %reshape.288, f32[]{:T(128)} %constant.36.clone.1), kind=kCustom, calls=%fused_computation.54 | custom fusion | bytes 4354564 | tf_op jit(solution)/shard_map/scatter | solution.py:115
  260.2 2.9 %copy.53 = f32[108,4,1440]{2,1,0:T(4,128)} copy(f32[108,4,1440]{0,2,1:T(8,128)S(1)} %bitcast.47) | data formatting | bytes 4976640 | tf_op jit(solution)/shard_map/reshape | solution.py:117
  (52 shorter events, 11.7 us)
Async XLA Ops:
  6.5 138.0 %all-gather.4.cloned.1.call-start = ((), (), s32[]{:S(2)}) async-start(), calls=%async_computation.2 | async-start | bytes 6823936 | tf_op jit(solution)/shard_map/all_gather | solution.py:104
  7.3 9.2 %copy-start = (s32[4,1440]{1,0:T(4,128)S(1)}, s32[4,1440]{1,0:T(4,128)}, u32[]{:S(2)}) copy-start(s32[4,1440]{1,0:T(4,128)} %param.11) | copy-start | bytes 69124
  9.9 6.6 %copy-start.2 = (s32[1,270]{1,0:T(1,128)S(1)}, s32[1,270]{1,0:T(1,128)}, u32[]{:S(2)}) copy-start(s32[1,270]{1,0:T(1,128)} %param.12) | copy-start | bytes 3244
  9.9 30.2 %copy-start.3 = (f32[48]{0:T(128)S(1)}, f32[48]{0:T(128)}, u32[]{:S(2)}) copy-start(f32[48]{0:T(128)} %param.8) | copy-start | bytes 580
  10.8 30.6 %collective-permute-start = (f32[108,1,1440]{2,0,1:T(8,128)}, f32[108,1,1440]{2,0,1:T(8,128)}, u32[]{:S(2)}, u32[]{:S(2)}) collective-permute-start(f32[108,1,1440]{2,0,1:T(8,128)} %get-tuple-element.21), channel_id=1, source_target_pairs={{0,16},{16,32},{32,48},{48,64},{64,80},{80,96},{96,112},{112,128},... | collective-permute-start | bytes 1866248 | tf_op jit(solution)/shard_map/ppermute | solution.py:27
  12.8 28.7 %collective-permute-start.1 = (f32[108,1,1440]{2,0,1:T(8,128)S(1)}, f32[108,1,1440]{2,0,1:T(8,128)}, u32[]{:S(2)}, u32[]{:S(2)}) collective-permute-start(f32[108,1,1440]{2,0,1:T(8,128)S(1)} %get-tuple-element.22), channel_id=1, source_target_pairs={{16,0},{32,16},{48,32},{64,48},{80,64},{96,80},{112,96},{128,112},... | collective-permute-start | bytes 1866248 | tf_op jit(solution)/shard_map/ppermute | solution.py:29
  45.4 18.7 %collective-permute-start.2 = (f32[108,1,1440]{2,0,1:T(8,128)S(1)}, f32[108,1,1440]{2,0,1:T(8,128)S(1)}, u32[]{:S(2)}, u32[]{:S(2)}) collective-permute-start(f32[108,1,1440]{2,0,1:T(8,128)S(1)} %get-tuple-element.15), channel_id=1, source_target_pairs={{0,16},{16,32},{32,48},{48,64},{64,80},{80,96},{96,112},{112,128},... | collective-permute-start | bytes 1866248 | tf_op jit(solution)/shard_map/ppermute | solution.py:27
  47.3 17.6 %collective-permute-start.3 = (f32[108,1,1440]{2,0,1:T(8,128)S(1)}, f32[108,1,1440]{2,0,1:T(8,128)S(1)}, u32[]{:S(2)}, u32[]{:S(2)}) collective-permute-start(f32[108,1,1440]{2,0,1:T(8,128)S(1)} %get-tuple-element.16), channel_id=1, source_target_pairs={{16,0},{32,16},{48,32},{64,48},{80,64},{96,80},{112,96},{128,112},... | collective-permute-start | bytes 1866248 | tf_op jit(solution)/shard_map/ppermute | solution.py:29
  67.7 12.4 %collective-permute-start.4 = (f32[108,1,1440]{2,0,1:T(8,128)S(1)}, f32[108,1,1440]{2,0,1:T(8,128)S(1)}, u32[]{:S(2)}, u32[]{:S(2)}) collective-permute-start(f32[108,1,1440]{2,0,1:T(8,128)S(1)} %get-tuple-element.9), channel_id=1, source_target_pairs={{0,16},{16,32},{32,48},{48,64},{64,80},{80,96},{96,112},{112,128},... | collective-permute-start | bytes 1866248 | tf_op jit(solution)/shard_map/ppermute | solution.py:27
  71.8 10.4 %collective-permute-start.5 = (f32[108,1,1440]{2,0,1:T(8,128)S(1)}, f32[108,1,1440]{2,0,1:T(8,128)S(1)}, u32[]{:S(2)}, u32[]{:S(2)}) collective-permute-start(f32[108,1,1440]{2,0,1:T(8,128)S(1)} %get-tuple-element.10), channel_id=1, source_target_pairs={{16,0},{32,16},{48,32},{64,48},{80,64},{96,80},{112,96},{128,112},... | collective-permute-start | bytes 1866248 | tf_op jit(solution)/shard_map/ppermute | solution.py:29
  100.5 7.6 %copy-start.1 = (s32[4,1440]{1,0:T(4,128)S(1)}, s32[4,1440]{1,0:T(4,128)}, u32[]{:S(2)}) copy-start(s32[4,1440]{1,0:T(4,128)} %param.10) | copy-start | bytes 69124
  100.5 38.4 %all-to-all-start = ((f32[108,16,270]{0,2,1:T(8,128)}), f32[108,16,270]{0,2,1:T(8,128)S(1)}, u32[]{:S(2)}, u32[]{:S(2)}) async-start(f32[108,16,270]{0,2,1:T(8,128)} %broadcast_select_fusion), calls=%async_computation | async-start | bytes 4456448 | tf_op jit(solution)/shard_map/all_to_all | solution.py:99
  169.9 9.3 %copy-start.4 = (u32[256]{0:T(256)S(1)}, u32[256]{0:T(256)}, u32[]{:S(2)}) copy-start(u32[256]{0:T(256)} %constant.101) | copy-start | bytes 3076
  169.9 58.5 %all-to-all-start.1 = ((f32[1728,1,270]{2,1,0:T(1,128)}), f32[1728,1,270]{2,1,0:T(1,128)S(1)}, u32[]{:S(2)}, u32[]{:S(2)}) async-start(f32[1728,1,270]{2,1,0:T(1,128)} %copy.50), calls=%async_computation.1 | async-start | bytes 5308416 | tf_op jit(solution)/shard_map/all_to_all | solution.py:109
Sparse Core Ops, SparseCore 0:
  9.2 55.3 all-gather.3
where the time goes:
time: 271 us; the launch traced here: 270 us
  local copies, waits for them, and re-layouts  77.5 us (29%)
  blocking collectives  70.9 us (26%)
  waiting for transfers between devices  49.2 us (18%)
  starting transfers between devices  33.3 us (12%)
  between operations  14.4 us (5%)
  other arithmetic  12.9 us (5%)
  matrix products  11.7 us (4%)
    unnamed x1, blocking collectives  47.6 us
    all_to_all x1, waiting for transfers between devices, body(): lax.all_to_all(outgoing, 'comp', split_axis=1, concat_axis=0, tiled=True)  28.4 us
    all_gather x1, blocking collectives, body(): lax.all_gather(owner_cells, 'comp', axis=0, tiled=True)  23.3 us
    scatter x1, local copies, waits for them, and re-layouts, body(): evolved = jnp.zeros((kdev, cells), jnp.float32).at[:, target.reshape(-1)]...  17.9 us
    ppermute x3, waiting for transfers between devices, padded_2(): lax.ppermute(tail, axis, [(i, (i + 1) % count) for i in range(ends)])  17.3 us
    unnamed x15, local copies, waits for them, and re-layouts  12.7 us
    all_to_all x3, local copies, waits for them, and re-layouts, body(): lax.all_to_all(updated.reshape(comps, 1, capacity), 'comp', split_axis=0,...  12.4 us
    dot_general x1, matrix products, body(): jnp.dot(lax.all_gather(coupling, 'band', axis=0, tiled=True), squared, pr...  11.7 us
  transfers between devices with their start and end apart: 9, of which 5 were waited for; matrix products, arithmetic and copies ran while one was open for 16% of the time, Pallas kernels for 0%

commit v1 on v0

v1 whole, which is shorter than its diff:
```python
import math

import jax
import jax.numpy as jnp
from jax import lax
from jax.experimental import pallas as pl
from jax.experimental.pallas import tpu as pltpu
from jax.sharding import PartitionSpec as P

DIRS = 36
FREQS = 48
COMPS = 1728
LON = 1440
ROWS = 4
NB = 16
KD = COMPS // NB
KP = 112
LP = 1536
KALL = NB * KP
QW = LP // 4
HALF = KALL // 2
CH = 16
NCH = KP // CH

first_lat = 30.0
step_time = 0.5
wind_gain = 0.6
damping = 0.4

MESH = pl.DeviceIdType.MESH
F32 = jnp.float32
BF16 = jnp.bfloat16


def lane_iota(shape):
    return lax.broadcasted_iota(jnp.int32, shape, 1)


def row_iota(shape):
    return lax.broadcasted_iota(jnp.int32, shape, 0)


def kernel(
    spec, coup, coef, aux, out,
    raw, f, hs, hr, mh, stage, S, C, tst, trv, eacc,
    load_sem, hs_sem, hr_sem, ms_sem, mr_sem, ss_sem, sr_sem, ts_sem, tr_sem,
    cs_sem, ring_sem, xy_sem, sib_sem,
):
    b = lax.axis_index("band")
    c = lax.axis_index("comp")
    core = b % 2
    y, x = c // 4, c % 4
    up = c < 8
    dirn = jnp.where(up, 1, -1)
    west = jnp.logical_or(c < 4, c >= 12)
    has_send = jnp.where(up, b < 15, b > 0)
    has_recv = jnp.where(up, b > 0, b < 15)
    to_band = (b + dirn + 16) % 16
    sib = b + 1 - 2 * core
    half = (x + y) % 2

    def row_of(i):
        return jnp.where(up, i, 3 - i)

    def load(i):
        return pltpu.make_async_copy(spec.at[:, row_of(i), :], raw.at[i], load_sem.at[i])

    for i in range(ROWS):
        load(i).start()

    barrier = pltpu.get_barrier_semaphore()

    @pl.loop(1, NB)
    def _(n):
        pl.semaphore_signal(barrier, inc=1, device_id={"comp": (c + n) % 16}, device_id_type=MESH)

    for n in (1, 2, 14, 15):
        pl.semaphore_signal(barrier, inc=1, device_id={"band": (b + n) % 16}, device_id_type=MESH)

    def pad_cols(v):
        n = v.shape[0]
        parts = []
        for s in range(NB):
            parts.append(v[:, s * KD : (s + 1) * KD])
            parts.append(jnp.zeros((n, KP - KD), F32))
        return jnp.concatenate(parts, axis=1)

    @pl.loop(0, NCH - 1)
    def _(g):
        rows = pl.ds(pl.multiple_of(g * CH, CH), CH)
        C[b, rows, :] = pad_cols(coup[rows, :].astype(F32)).astype(BF16)

    tail = pad_cols(coup[KD - 12 :, :].astype(F32))
    tail = jnp.concatenate([tail, jnp.zeros((4, KALL), F32)], axis=0)
    spot = lane_iota((CH, KALL)) % KP
    ones = jnp.logical_and(spot >= KD, spot < KD + 3)
    ones = jnp.logical_and(ones, row_iota((CH, KALL)) == 12)
    C[b, pl.ds(KP - CH, CH), :] = jnp.where(ones, 1.0, tail).astype(BF16)

    for i in range(ROWS):
        load(i).wait()

    pl.semaphore_wait(barrier, NB - 1 + 4)

    mask_copy = pltpu.make_async_remote_copy(
        src_ref=aux.at[pl.ds(2, 2)], dst_ref=mh, send_sem=ms_sem, recv_sem=mr_sem,
        device_id={"band": to_band}, device_id_type=MESH,
    )

    def halo(j):
        rows = pl.ds(pl.multiple_of(j * CH, CH), CH)
        return pltpu.make_async_remote_copy(
            src_ref=hs.at[:, rows, :], dst_ref=hr.at[:, rows, :],
            send_sem=hs_sem, recv_sem=hr_sem.at[j],
            device_id={"band": to_band}, device_id_type=MESH,
        )

    @pl.when(has_send)
    def _():
        mask_copy.start()

    def build(j, count):
        rows = pl.ds(pl.multiple_of(j * CH, CH), CH)
        for i in range(ROWS):
            v = raw[i, pl.ds(pl.multiple_of(j * CH, CH), count), :]
            v = jnp.concatenate([v, v[:, :48], v[:, LON - 48 :]], axis=1)
            if count < CH:
                v = jnp.concatenate([v, jnp.zeros((CH - count, LP), F32)], axis=0)
            f[3 + i, rows, :] = v
            if i > 0:
                hs[i - 1, rows, :] = v.astype(BF16)

        @pl.when(has_send)
        def _():
            halo(j).start()

    @pl.loop(0, NCH - 1)
    def _(j):
        build(j, CH)

    build(NCH - 1, KD - CH * (NCH - 1))

    mine = pl.ds(pl.multiple_of(half * HALF, 128), HALF)
    theirs = pl.ds(pl.multiple_of((1 - half) * HALF, 128), HALF)

    def ring(block, step, n):
        return pltpu.make_async_remote_copy(
            src_ref=C.at[block, :, mine], dst_ref=C.at[block, :, mine],
            send_sem=cs_sem, recv_sem=ring_sem.at[n],
            device_id={"band": (b + step + 32) % 16}, device_id_type=MESH,
        )

    xy = (
        y * 4 + (x + 1) % 4,
        y * 4 + (x + 3) % 4,
        ((y + 1) % 4) * 4 + x,
        ((y + 3) % 4) * 4 + x,
    )

    def spread(block, at):
        for k, (lo, cnt) in enumerate(((0, 32), (32, 32), (64, 32), (96, 16))):
            piece = C.at[block, pl.ds(lo, cnt), mine]
            pltpu.make_async_remote_copy(
                src_ref=piece, dst_ref=piece, send_sem=cs_sem, recv_sem=xy_sem.at[at],
                device_id={"comp": xy[k]}, device_id_type=MESH,
            ).start()

    def to_sib(block, cols, n):
        return pltpu.make_async_remote_copy(
            src_ref=C.at[block, :, cols], dst_ref=C.at[block, :, cols],
            send_sem=cs_sem, recv_sem=sib_sem.at[n],
            device_id={"band": sib}, device_id_type=MESH,
        )

    events = ((1, 1), (-1, 1), (1, 2), (-1, 2), (1, 3), (1, 4), (1, 5))
    last = {1: 5, -1: 2}

    def block_of(side, s, base=None):
        base = b if base is None else base
        return (base + 2 * side * s * dirn + 32) % 16

    def distance(side, s):
        return (side * s * dirn + 8) % 8 - 1

    def ring_event(n):
        side, s = events[n]
        block = block_of(side, s)
        ring(block, 0, n).wait_recv()
        if s < last[side]:
            ring(block, -2 * side * dirn, events.index((side, s + 1))).start()
        spread(block, distance(side, s))
        to_sib(block, mine, n).start()

    def xy_event(n):
        side, s = events[n]
        block = block_of(side, s)
        whole = C.at[block, :, theirs]
        pltpu.make_async_copy(whole, whole, xy_sem.at[distance(side, s)]).wait()
        to_sib(block, theirs, n).start()

    ring(b, -2 * dirn, 0).start()
    ring(b, 2 * dirn, 1).start()
    to_sib(b, pl.ds(0, KALL), 7).start()

    def advect(rows, shift):
        cols = [coef[rows, p : p + 1] for p in range(8)]
        for s in range(3):
            for p in range(6, s, -1):
                v = f[p, rows, :]
                moved = v - cols[p] * (v - pltpu.roll(v, shift, 1)) - cols[7] * (v - f[p - 1, rows, :])
                f[p, rows, :] = moved * (mh[p - 1] if p < 3 else aux[p - 3])

    eacc[...] = jnp.zeros_like(eacc)

    @pl.when(has_recv)
    def _():
        mask_copy.wait_recv()

    @pl.when(jnp.logical_not(has_recv))
    def _():
        mh[...] = jnp.zeros_like(mh)

    def send_squares(j):
        rows = pl.ds(pl.multiple_of(j * CH, CH), CH)
        place = pl.ds(pl.multiple_of(c * KP + j * CH, CH), CH)

        @pl.loop(1, NB)
        def _(n):
            to = (c + n) % 16
            pltpu.make_async_remote_copy(
                src_ref=stage.at[to, rows, :], dst_ref=S.at[place, :],
                send_sem=ss_sem, recv_sem=sr_sem,
                device_id={"comp": to}, device_id_type=MESH,
            ).start()

    def chunk(j, final):
        rows = pl.ds(pl.multiple_of(j * CH, CH), CH)

        @pl.when(has_recv)
        def _():
            halo(j).wait_recv()
            for p in range(3):
                f[p, rows, :] = hr[p, rows, :].astype(F32)

        @pl.when(jnp.logical_not(has_recv))
        def _():
            for p in range(3):
                f[p, rows, :] = jnp.zeros((CH, LP), F32)

        @pl.when(west)
        def _():
            for h in range(2):
                advect(pl.ds(pl.multiple_of(j * CH + 8 * h, 8), 8), 1)

        @pl.when(jnp.logical_not(west))
        def _():
            for h in range(2):
                advect(pl.ds(pl.multiple_of(j * CH + 8 * h, 8), 8), LP - 1)

        for i in range(ROWS):
            for q in range(4):
                lanes = pl.ds(q * QW, QW)
                v = f[3 + i, rows, lanes]
                sq = v * v
                e = eacc[i, :, lanes] + v[:8] + v[8:]
                if final:
                    total = jnp.sum(e, axis=0, keepdims=True)
                    hi = total.astype(BF16).astype(F32)
                    mid = (total - hi).astype(BF16).astype(F32)
                    lo = total - hi - mid
                    at = row_iota((CH, QW))
                    sq = jnp.where(at == 12, hi, jnp.where(at == 13, mid, jnp.where(at == 14, lo, sq)))
                else:
                    eacc[i, :, lanes] = e
                stage[4 * row_of(i) + q, rows, :] = sq.astype(BF16)
        send_squares(j)

    for j in range(NCH - 1):
        chunk(j, False)
        ring_event(j)
        if 0 < j < 5:
            xy_event(j - 1)
    chunk(NCH - 1, True)
    ring_event(NCH - 1)
    for n in range(4, NCH):
        xy_event(n)

    S[pl.ds(pl.multiple_of(c * KP, CH), KP), :] = stage[c]
    for n in range(NCH):
        side, s = events[n]
        block = block_of(side, s, sib)
        to_sib(block, pl.ds(0, KALL), n).wait_recv()
    to_sib(sib, pl.ds(0, KALL), 7).wait_recv()
    rest = S.at[pl.ds(0, (NB - 1) * KP), :]
    pltpu.make_async_copy(rest, rest, sr_sem).wait()

    def back(to):
        return pltpu.make_async_remote_copy(
            src_ref=tst.at[to], dst_ref=trv.at[c], send_sem=ts_sem, recv_sem=tr_sem.at[c],
            device_id={"comp": to}, device_id_type=MESH,
        )

    def code(t):
        at = row_iota((KP, QW))
        mean = t[KD : KD + 1] * (1.0 / COMPS)
        t = jnp.maximum(t, -6.0)
        top = jnp.max(jnp.where(at < KD, jnp.abs(t), 0.0), axis=0, keepdims=True)
        power = jnp.ceil(jnp.log2(jnp.maximum(top, 1e-12)) + 0.01)
        scaled = t * (32000.0 * jnp.exp2(-power))
        hi = jnp.floor(mean * 16000.0)
        lo = (mean * 16000.0 - hi) * 32000.0
        scaled = jnp.where(at < KD, scaled, jnp.where(at == KD, power, jnp.where(at == KD + 1, hi, lo)))
        return jnp.round(scaled).astype(jnp.int32).astype(jnp.int16)

    @pl.loop(0, NB // 2)
    def _(n):
        pair = (c // 2 + n) % 8
        lhs = C[pl.ds(pair * 2, 2)].reshape(2 * KP, KALL)
        t = jnp.dot(lhs, S[...], preferred_element_type=F32)
        for k in range(2):
            to = pair * 2 + k
            tst[to] = code(t[k * KP : (k + 1) * KP])

            @pl.when(to != c)
            def _():
                back(to).start()

    trv[c] = tst[c]

    for i in range(ROWS):
        r = row_of(i)
        for q in range(4):
            o = 4 * r + q
            lanes = pl.ds(q * QW, QW)

            @pl.when(o != c)
            def _():
                pltpu.make_async_copy(tst.at[o], trv.at[o], tr_sem.at[o]).wait()

            info = trv[o, pl.ds(KP - CH, CH), :].astype(jnp.int32).astype(F32)
            scale = jnp.exp2(info[12:13]) * (step_time / 32000.0)
            energy = (info[13:14] + info[14:15] * (1.0 / 32000.0)) * (step_time * damping / 16000.0)
            mask = aux[i, :, lanes]
            cosw = aux[4 + i, :, lanes]
            sinw = aux[8 + i, :, lanes]
            width = min(QW, LON - q * QW)

            def update(j, count):
                rows = pl.ds(pl.multiple_of(j * CH, CH), CH)
                t = trv[o, rows, :].astype(jnp.int32).astype(F32)
                v = f[3 + i, rows, lanes]
                facing = jnp.maximum(coef[rows, 8:9] * cosw + coef[rows, 9:10] * sinw, 0.0)
                new = v + ((step_time * wind_gain) * facing - energy) * v + t * scale
                new = jnp.maximum(new, 0.0) * mask
                out[r, pl.ds(pl.multiple_of(j * CH, CH), count), pl.ds(q * QW, width)] = new[:count, :width]

            @pl.loop(0, NCH - 1)
            def _(j):
                update(j, CH)

            update(NCH - 1, KD - CH * (NCH - 1))

    @pl.when(has_send)
    def _():
        mask_copy.wait_send()
        pltpu.make_async_copy(hs, hs, hs_sem).wait()

    sent = C.at[pl.ds(0, 15)]
    pltpu.make_async_copy(sent, sent, cs_sem).wait()
    pltpu.make_async_copy(rest, rest, ss_sem).wait()
    tsent = tst.at[pl.ds(0, 15)]
    pltpu.make_async_copy(tsent, tsent, ts_sem).wait()


def body(spectrum, group_courant, coupling, wind_dir, sea_mask, owner_cells, owner_counts):
    b = lax.axis_index("band")
    c = lax.axis_index("comp")
    up = c < 8
    local = jnp.arange(KP, dtype=jnp.int32)
    index = c * KD + local
    freq = index % FREQS
    dirn = index // FREQS
    picker = (freq[:, None] == jnp.arange(FREQS, dtype=jnp.int32)[None, :]).astype(F32)
    speed = jnp.sum(picker * group_courant[None, :], axis=1)
    speed = jnp.where(local < KD, speed, 0.0)
    theta = 2.0 * math.pi / DIRS * dirn.astype(F32)
    plane = jnp.arange(7, dtype=jnp.int32)
    row = b * ROWS + jnp.where(up, plane - 3, 6 - plane)
    latitude = (first_lat + 0.25 * (row.astype(F32) + 0.5)) * (math.pi / 180.0)
    cosd, sind = jnp.cos(theta)[:, None], jnp.sin(theta)[:, None]
    cross_x = jnp.abs(speed[:, None] * cosd) / jnp.cos(latitude)[None, :]
    cross_y = jnp.abs(speed[:, None] * sind)
    coef = jnp.concatenate([cross_x, cross_y, cosd, sind, jnp.zeros((KP, 6), F32)], axis=1)
    angle = 2.0 * math.pi / DIRS * wind_dir.astype(F32)
    aux = jnp.concatenate([
        jnp.where(up, v, v[::-1]) for v in (sea_mask.astype(F32), jnp.cos(angle), jnp.sin(angle))
    ], axis=0)
    aux = jnp.concatenate([aux, aux[:, :48], aux[:, LON - 48 :]], axis=1).reshape(12, 1, LP)

    vmem = pl.BlockSpec(memory_space=pltpu.VMEM)
    dma = pltpu.SemaphoreType.DMA
    out = pl.pallas_call(
        kernel,
        out_shape=jax.ShapeDtypeStruct((ROWS, KD, LON), F32),
        in_specs=[pl.BlockSpec(memory_space=pl.ANY), vmem, vmem, vmem],
        out_specs=vmem,
        scratch_shapes=[
            pltpu.VMEM((ROWS, KD, LON), F32),
            pltpu.VMEM((7, KP, LP), F32),
            pltpu.VMEM((3, KP, LP), BF16),
            pltpu.VMEM((3, KP, LP), BF16),
            pltpu.VMEM((2, 1, LP), F32),
            pltpu.VMEM((NB, KP, QW), BF16),
            pltpu.VMEM((KALL, QW), BF16),
            pltpu.VMEM((NB, KP, KALL), BF16),
            pltpu.VMEM((NB, KP, QW), jnp.int16),
            pltpu.VMEM((NB, KP, QW), jnp.int16),
            pltpu.VMEM((ROWS, 8, LP), F32),
            dma((ROWS,)), dma, dma((NCH,)), dma, dma, dma, dma, dma, dma((NB,)),
            dma, dma((7,)), dma((7,)), dma((8,)),
        ],
        compiler_params=pltpu.CompilerParams(
            collective_id=0, has_side_effects=True, vmem_limit_bytes=56 * 2**20
        ),
        cost_estimate=pl.CostEstimate(
            flops=2 * KALL * KALL * QW, bytes_accessed=12 * 2**20, transcendentals=0
        ),
    )(spectrum, coupling, coef, aux)
    return jnp.transpose(out, (1, 0, 2))


def solution(mesh):
    return jax.shard_map(
        body,
        mesh=mesh,
        in_specs=(
            P("comp", "band", None),
            P(),
            P("band", None),
            P("band", None),
            P("band", None),
            P(("band", "comp"), None),
            P(("band", "comp")),
        ),
        out_specs=P("comp", "band", None),
        check_vma=False,
    )
```

time: 271 us -> 101 us (0.37)
  the two profiles are of different devices: /device:TPU:34 before, /device:TPU:1 now
where the time goes in v1:
time: 101 us; the launch traced here: 99.8 us
  Pallas kernels  87.6 us (87%)
  local copies, waits for them, and re-layouts  7.51 us (7%)
  other arithmetic  4.61 us (5%)
    pallas_call x1, Pallas kernels, body(): pl.pallas_call(kernel, out_shape=jax.ShapeDtypeStruct((ROWS, KD, LON), F3...  87.6 us
    transpose x1, local copies, waits for them, and re-layouts, body(): return jnp.transpose(out, (1, 0, 2))  4.99 us

profile of v1, /device:TPU:1, one launch (start us, length us, event | category | flops | bytes accessed | tf_op | source)
XLA Modules:
  0.0 99.8 jit_solution(13409977602491534959)
XLA Ops:
  0.0 0.1 fusion.11
  0.1 0.7 select_reduce_fusion
  0.9 0.1 fusion.9
  0.9 0.1 fusion.8
  1.0 0.1 broadcast_divide_fusion
  1.1 0.8 convert_element_type.40
  1.9 0.3 rev.9
  2.2 0.9 fusion.1
  3.1 0.3 rev.10
  3.4 0.9 broadcast_select_fusion.1
  4.3 0.3 rev.11
  4.7 0.9 broadcast_select_fusion
  5.6 0.1 fusion.12
  5.7 0.1 concatenate.11
  5.8 0.7 reshape.99.aux
  6.5 0.7 copy.10.coef
  7.2 87.6 %shard_map.55 = f32[4,108,1440]{2,1,0:T(8,128)} custom-call(f32[108,4,1440]{2,1,0:T(4,128)} %spec.1, bf16[108,1728]{1,0:T(8,128)(2,1)} %coup.1, f32[112,16]{1,0:T(8,128)} %copy.10.coef, f32[12,1,1536]{2,1,0:T(1,128)} %reshape.99.aux), custom_call_target="tpu_custom_call" | custom-call | flops 2466250752 | bytes 12582912 | tf_op jit(solution)/shard_map/pallas_call | solution.py:402
  94.8 5.0 %copy.11 = f32[108,4,1440]{2,1,0:T(4,128)} copy(f32[108,4,1440]{2,0,1:T(8,128)} %bitcast.5) | data formatting | bytes 4976640 | tf_op jit(solution)/shard_map/transpose | solution.py:429
  (5 shorter events, 0.1 us)

commit v2 on v1

v2 whole, which is shorter than its diff:
```python
import math

import jax
import jax.numpy as jnp
from jax import lax
from jax.experimental import pallas as pl
from jax.experimental.pallas import tpu as pltpu
from jax.sharding import PartitionSpec as P

DIRS = 36
FREQS = 48
COMPS = 1728
LON = 1440
ROWS = 4
NB = 16
KD = COMPS // NB
KP = 112
LP = 1536
KALL = NB * KP
QW = LP // 4
HALF = KALL // 2
CH = 16
NCH = KP // CH

first_lat = 30.0
step_time = 0.5
wind_gain = 0.6
damping = 0.4

MESH = pl.DeviceIdType.MESH
F32 = jnp.float32
BF16 = jnp.bfloat16


def lane_iota(shape):
    return lax.broadcasted_iota(jnp.int32, shape, 1)


def row_iota(shape):
    return lax.broadcasted_iota(jnp.int32, shape, 0)


def kernel(
    spec, gc, coup, wind, sea, out,
    raw, f, hs, hr, coef, aux, mrow, mh, mask_h, stage, S, C, tst, trv, eacc,
    load_sem, hs_sem, hr_sem, ms_sem, mr_sem, ss_sem, sr_sem, ts_sem, tr_sem,
    cs_sem, ring_sem, xy_sem, sib_sem, out_sem,
):
    b = lax.axis_index("band")
    c = lax.axis_index("comp")
    z, core = b // 2, b % 2
    y, x = c // 4, c % 4
    up = c < 8
    dirn = jnp.where(up, 1, -1)
    west = jnp.logical_or(c < 4, c >= 12)
    has_send = jnp.where(up, b < 15, b > 0)
    has_recv = jnp.where(up, b > 0, b < 15)
    to_band = (b + dirn + 16) % 16
    sib = b + 1 - 2 * core
    half = (x + y) % 2

    def row_of(i):
        return jnp.where(up, i, 3 - i)

    def rows_at(j, count=CH):
        return pl.ds(pl.multiple_of(j * CH, CH), count)

    def load(j, i):
        count = CH if j < NCH - 1 else KD - CH * (NCH - 1)
        return pltpu.make_async_copy(
            spec.at[pl.ds(j * CH, count), row_of(i), :],
            raw.at[i, pl.ds(j * CH, count), :],
            load_sem.at[j, i],
        )

    for j in range(NCH):
        for i in range(ROWS):
            load(j, i).start()

    barrier = pltpu.get_barrier_semaphore()

    @pl.loop(1, NB)
    def _(n):
        pl.semaphore_signal(barrier, inc=1, device_id={"comp": (c + n) % 16}, device_id_type=MESH)

    for n in (1, 2, 14, 15):
        pl.semaphore_signal(barrier, inc=1, device_id={"band": (b + n) % 16}, device_id_type=MESH)

    def pad_cols(v):
        n = v.shape[0]
        parts = []
        for s in range(NB):
            parts.append(v[:, s * KD : (s + 1) * KD])
            parts.append(jnp.zeros((n, KP - KD), F32))
        return jnp.concatenate(parts, axis=1)

    @pl.loop(0, NCH - 1)
    def _(g):
        C[b, rows_at(g), :] = pad_cols(coup[rows_at(g), :].astype(F32)).astype(BF16)

    tail = pad_cols(coup[KD - 12 :, :].astype(F32))
    tail = jnp.concatenate([tail, jnp.zeros((4, KALL), F32)], axis=0)
    spot = lane_iota((CH, KALL)) % KP
    ones = jnp.logical_and(spot >= KD, spot < KD + 3)
    ones = jnp.logical_and(ones, row_iota((CH, KALL)) == 12)
    C[b, pl.ds(KP - CH, CH), :] = jnp.where(ones, 1.0, tail).astype(BF16)

    def wrap(v):
        return jnp.concatenate([v, v[:, :48], v[:, LON - 48 :]], axis=1)

    seas = wrap(sea[...].astype(F32))
    angle = 2.0 * math.pi / DIRS * wind[...].astype(F32)
    cosw, sinw = wrap(jnp.cos(angle)), wrap(jnp.sin(angle))
    for r in range(ROWS):
        for k, v in enumerate((seas, cosw, sinw)):
            aux[4 * k + row_of(r)] = jnp.broadcast_to(v[r : r + 1], (8, LP))
        mrow[row_of(r)] = seas[r : r + 1]

    pl.semaphore_wait(barrier, NB - 1 + 4)

    mask_copy = pltpu.make_async_remote_copy(
        src_ref=mrow.at[pl.ds(2, 2)], dst_ref=mh, send_sem=ms_sem, recv_sem=mr_sem,
        device_id={"band": to_band}, device_id_type=MESH,
    )

    def halo(j):
        rows = rows_at(j)
        return pltpu.make_async_remote_copy(
            src_ref=hs.at[:, rows, :], dst_ref=hr.at[:, rows, :],
            send_sem=hs_sem, recv_sem=hr_sem.at[j],
            device_id={"band": to_band}, device_id_type=MESH,
        )

    mine = pl.ds(pl.multiple_of(half * HALF, 128), HALF)
    theirs = pl.ds(pl.multiple_of((1 - half) * HALF, 128), HALF)

    def ring(block, step, n):
        return pltpu.make_async_remote_copy(
            src_ref=C.at[block, :, mine], dst_ref=C.at[block, :, mine],
            send_sem=cs_sem, recv_sem=ring_sem.at[n],
            device_id={"band": (b + step + 32) % 16}, device_id_type=MESH,
        )

    xy = (
        y * 4 + (x + 1) % 4,
        y * 4 + (x + 3) % 4,
        ((y + 1) % 4) * 4 + x,
        ((y + 3) % 4) * 4 + x,
    )

    def spread(block, at):
        for k, (lo, cnt) in enumerate(((0, 32), (32, 32), (64, 32), (96, 16))):
            piece = C.at[block, pl.ds(lo, cnt), mine]
            pltpu.make_async_remote_copy(
                src_ref=piece, dst_ref=piece, send_sem=cs_sem, recv_sem=xy_sem.at[at],
                device_id={"comp": xy[k]}, device_id_type=MESH,
            ).start()

    def to_sib(block, cols, n):
        return pltpu.make_async_remote_copy(
            src_ref=C.at[block, :, cols], dst_ref=C.at[block, :, cols],
            send_sem=cs_sem, recv_sem=sib_sem.at[n],
            device_id={"band": sib}, device_id_type=MESH,
        )

    events = ((1, 1), (-1, 1), (1, 2), (-1, 2), (1, 3), (-1, 3), (1, 4))
    last = {1: 4, -1: 3}

    def block_of(side, s, base=None):
        base = b if base is None else base
        return (base + 2 * side * s * dirn + 32) % 16

    def distance(side, s):
        return (side * s * dirn + 8) % 8 - 1

    def ring_event(n):
        side, s = events[n]
        block = block_of(side, s)
        ring(block, 0, n).wait_recv()
        if s < last[side]:
            ring(block, -2 * side * dirn, events.index((side, s + 1))).start()
        spread(block, distance(side, s))
        to_sib(block, mine, n).start()

    def xy_event(n):
        side, s = events[n]
        block = block_of(side, s)
        whole = C.at[block, :, theirs]
        pltpu.make_async_copy(whole, whole, xy_sem.at[distance(side, s)]).wait()
        to_sib(block, theirs, n).start()

    def sib_event(n):
        side, s = events[n]
        to_sib(block_of(side, s, sib), pl.ds(0, KALL), n).wait_recv()

    ring(b, -2 * dirn, 0).start()

    @pl.when(has_send)
    def _():
        mask_copy.start()

    for j in range(NCH):
        count = CH if j < NCH - 1 else KD - CH * (NCH - 1)
        for i in range(ROWS):
            load(j, i).wait()
            v = wrap(raw[i, pl.ds(j * CH, count), :])
            if count < CH:
                v = jnp.concatenate([v, jnp.zeros((CH - count, LP), F32)], axis=0)
            f[3 + i, pl.ds(j * CH, CH), :] = v
            if i > 0:
                hs[i - 1, pl.ds(j * CH, CH), :] = v.astype(BF16)

        @pl.when(has_send)
        def _():
            halo(j).start()

    ring(b, 2 * dirn, 1).start()
    to_sib(b, pl.ds(0, KALL), 7).start()

    shape = (KP, 128)
    comp = (row_iota(shape) + c * KD).astype(F32)
    direction = jnp.floor((comp + 0.5) * (1.0 / FREQS))
    picked = lane_iota(shape).astype(F32) == comp - FREQS * direction
    speeds = jnp.concatenate([gc[...], jnp.zeros((1, 128 - FREQS), F32)], axis=1)
    speed = jnp.sum(jnp.where(picked, speeds, 0.0), axis=1, keepdims=True)
    speed = jnp.where(row_iota(shape) < KD, speed, 0.0)
    theta = 2.0 * math.pi / DIRS * direction
    cosd, sind = jnp.cos(theta), jnp.sin(theta)
    coef[8] = cosd
    coef[9] = sind
    coef[7] = jnp.abs(speed * sind)
    along = jnp.abs(speed * cosd)
    plane = row_iota((8, 128))
    row = (b * ROWS + jnp.where(up, plane - 3, 6 - plane)).astype(F32)
    inverse = 1.0 / jnp.cos((first_lat + 0.25 * (row + 0.5)) * (math.pi / 180.0))
    for p in range(7):
        coef[p] = along * inverse[p : p + 1]

    def wide(v, n):
        return jnp.concatenate([v] * n, axis=1)

    def advect(rows, shift):
        cols = [wide(coef[p, rows, :], LP // 128) for p in range(8)]
        for s in range(3):
            for p in range(6, s, -1):
                v = f[p, rows, :]
                moved = v - cols[p] * (v - pltpu.roll(v, shift, 1)) - cols[7] * (v - f[p - 1, rows, :])
                f[p, rows, :] = moved * (mask_h[p - 1] if p < 3 else aux[p - 3])

    eacc[...] = jnp.zeros_like(eacc)

    @pl.when(has_recv)
    def _():
        mask_copy.wait_recv()
        for p in range(2):
            mask_h[p] = jnp.broadcast_to(mh[p], (8, LP))

    @pl.when(jnp.logical_not(has_recv))
    def _():
        mask_h[...] = jnp.zeros_like(mask_h)

    @pl.loop(0, NCH)
    def _(j):
        rows = rows_at(j)

        @pl.when(has_recv)
        def _():
            halo(j).wait_recv()
            for p in range(3):
                f[p, rows, :] = hr[p, rows, :].astype(F32)

        @pl.when(jnp.logical_not(has_recv))
        def _():
            for p in range(3):
                f[p, rows, :] = jnp.zeros((CH, LP), F32)

        @pl.when(west)
        def _():
            for h in range(2):
                advect(pl.ds(pl.multiple_of(j * CH + 8 * h, 8), 8), 1)

        @pl.when(jnp.logical_not(west))
        def _():
            for h in range(2):
                advect(pl.ds(pl.multiple_of(j * CH + 8 * h, 8), 8), LP - 1)

        for i in range(ROWS):
            for q in range(4):
                lanes = pl.ds(q * QW, QW)
                v = f[3 + i, rows, lanes]
                eacc[i, :, lanes] = eacc[i, :, lanes] + v[:8] + v[8:]
                stage[4 * row_of(i) + q, rows, :] = (v * v).astype(BF16)

        @pl.when(j == NCH - 1)
        def _():
            at = row_iota((CH, QW))
            for i in range(ROWS):
                for q in range(4):
                    lanes = pl.ds(q * QW, QW)
                    total = jnp.sum(eacc[i, :, lanes], axis=0, keepdims=True)
                    hi = total.astype(BF16).astype(F32)
                    mid = (total - hi).astype(BF16).astype(F32)
                    lo = total - hi - mid
                    sq = stage[4 * row_of(i) + q, rows, :].astype(F32)
                    sq = jnp.where(at == 12, hi, jnp.where(at == 13, mid, jnp.where(at == 14, lo, sq)))
                    stage[4 * row_of(i) + q, rows, :] = sq.astype(BF16)

        place = pl.ds(pl.multiple_of(c * KP + j * CH, CH), CH)

        @pl.loop(1, NB)
        def _(n):
            to = (c + n) % 16
            pltpu.make_async_remote_copy(
                src_ref=stage.at[to, rows, :], dst_ref=S.at[place, :],
                send_sem=ss_sem, recv_sem=sr_sem,
                device_id={"comp": to}, device_id_type=MESH,
            ).start()

        @pl.when(j == 2)
        def _():
            ring_event(0)

        @pl.when(j == 3)
        def _():
            ring_event(1)

        @pl.when(j == 4)
        def _():
            ring_event(2)
            xy_event(0)
            xy_event(1)

        @pl.when(j == 5)
        def _():
            ring_event(3)

    S[pl.ds(pl.multiple_of(c * KP, CH), KP), :] = stage[c]
    xy_event(2)
    xy_event(3)
    ring_event(4)
    for n in (7, 0, 1, 2, 3):
        if n == 7:
            to_sib(sib, pl.ds(0, KALL), 7).wait_recv()
        else:
            sib_event(n)
    rest = S.at[pl.ds(0, (NB - 1) * KP), :]
    pltpu.make_async_copy(rest, rest, sr_sem).wait()

    def back(to):
        return pltpu.make_async_remote_copy(
            src_ref=tst.at[to], dst_ref=trv.at[c], send_sem=ts_sem, recv_sem=tr_sem.at[c],
            device_id={"comp": to}, device_id_type=MESH,
        )

    def code(t):
        at = row_iota((KP, QW))
        mean = t[KD : KD + 1] * (1.0 / COMPS)
        t = jnp.maximum(t, -6.0)
        top = jnp.max(jnp.where(at < KD, jnp.abs(t), 0.0), axis=0, keepdims=True)
        power = jnp.ceil(jnp.log2(jnp.maximum(top, 1e-12)) + 0.01)
        scaled = t * (32000.0 * jnp.exp2(-power))
        hi = jnp.floor(mean * 16000.0)
        lo = (mean * 16000.0 - hi) * 32000.0
        scaled = jnp.where(at < KD, scaled, jnp.where(at == KD, power, jnp.where(at == KD + 1, hi, lo)))
        return jnp.round(scaled).astype(jnp.int32).astype(jnp.int16)

    def multiply(chip):
        lhs = C[pl.ds(chip * 2, 2)].reshape(2 * KP, KALL)
        t = jnp.dot(lhs, S[...], preferred_element_type=F32)
        for k in range(2):
            to = chip * 2 + k
            tst[to] = code(t[k * KP : (k + 1) * KP])

            @pl.when(to != c)
            def _():
                back(to).start()

    @pl.loop(0, 5)
    def _(n):
        multiply((z + (n + c) % 5 + 6) % 8)

        @pl.when(n == 0)
        def _():
            ring_event(5)

        @pl.when(n == 1)
        def _():
            ring_event(6)

        @pl.when(n == 2)
        def _():
            xy_event(4)
            xy_event(5)

        @pl.when(n == 3)
        def _():
            xy_event(6)

    for n in (4, 5, 6):
        sib_event(n)

    @pl.loop(0, 3)
    def _(n):
        multiply((z + (n + c) % 3 + 3) % 8)

    trv[c] = tst[c]

    def finish(i, q, width):
        r = row_of(i)
        o = 4 * r + q
        lanes = pl.ds(pl.multiple_of(q * QW, 128), QW)
        final_lanes = pl.ds(pl.multiple_of(q * QW, 128), width)

        @pl.when(o != c)
        def _():
            pltpu.make_async_copy(tst.at[o], trv.at[o], tr_sem.at[o]).wait()

        info = trv[o, pl.ds(KP - CH, CH), :].astype(jnp.int32).astype(F32)[8:]
        scale = jnp.broadcast_to(jnp.exp2(info)[4:5] * (step_time / 32000.0), (8, QW))
        energy = info[5:6] + info[6:7] * (1.0 / 32000.0)
        energy = jnp.broadcast_to(energy * (step_time * damping / 16000.0), (8, QW))
        mask = aux[i, :, lanes]
        cosw = aux[4 + i, :, lanes] * (step_time * wind_gain)
        sinw = aux[8 + i, :, lanes] * (step_time * wind_gain)
        for j in range(NCH):
            t = trv[o, pl.ds(j * CH, CH), :].astype(jnp.int32).astype(F32)
            for h in range(2):
                rows = pl.ds(j * CH + 8 * h, 8)
                v = f[3 + i, rows, lanes]
                facing = wide(coef[8, rows, :], 3) * cosw + wide(coef[9, rows, :], 3) * sinw
                new = v + (jnp.maximum(facing, 0.0) - energy) * v + t[8 * h : 8 * h + 8] * scale
                new = jnp.maximum(new, 0.0) * mask
                count = min(8, KD - (j * CH + 8 * h))
                raw[i, pl.ds(j * CH + 8 * h, count), final_lanes] = new[:count, :width]

    def result(i):
        return pltpu.make_async_copy(raw.at[i], out.at[:, row_of(i), :], out_sem.at[i])

    @pl.loop(0, ROWS)
    def _(i):
        @pl.loop(0, 3)
        def _(q):
            finish(i, q, QW)

        finish(i, 3, LON - 3 * QW)
        result(i).start()

    @pl.when(has_send)
    def _():
        mask_copy.wait_send()
        pltpu.make_async_copy(hs, hs, hs_sem).wait()

    sent = C.at[pl.ds(0, 15)]
    pltpu.make_async_copy(sent, sent, cs_sem).wait()
    pltpu.make_async_copy(rest, rest, ss_sem).wait()
    tsent = tst.at[pl.ds(0, 15)]
    pltpu.make_async_copy(tsent, tsent, ts_sem).wait()
    for i in range(ROWS):
        result(i).wait()


def body(spectrum, group_courant, coupling, wind_dir, sea_mask, owner_cells, owner_counts):
    vmem = pl.BlockSpec(memory_space=pltpu.VMEM)
    hbm = pl.BlockSpec(memory_space=pl.ANY)
    dma = pltpu.SemaphoreType.DMA
    return pl.pallas_call(
        kernel,
        out_shape=jax.ShapeDtypeStruct((KD, ROWS, LON), F32),
        in_specs=[hbm, vmem, vmem, vmem, vmem],
        out_specs=hbm,
        scratch_shapes=[
            pltpu.VMEM((ROWS, KD, LON), F32),
            pltpu.VMEM((7, KP, LP), F32),
            pltpu.VMEM((3, KP, LP), BF16),
            pltpu.VMEM((3, KP, LP), BF16),
            pltpu.VMEM((10, KP, 128), F32),
            pltpu.VMEM((12, 8, LP), F32),
            pltpu.VMEM((ROWS, 1, LP), F32),
            pltpu.VMEM((2, 1, LP), F32),
            pltpu.VMEM((2, 8, LP), F32),
            pltpu.VMEM((NB, KP, QW), BF16),
            pltpu.VMEM((KALL, QW), BF16),
            pltpu.VMEM((NB, KP, KALL), BF16),
            pltpu.VMEM((NB, KP, QW), jnp.int16),
            pltpu.VMEM((NB, KP, QW), jnp.int16),
            pltpu.VMEM((ROWS, 8, LP), F32),
            dma((NCH, ROWS)), dma, dma((NCH,)), dma, dma, dma, dma, dma, dma((NB,)),
            dma, dma((7,)), dma((7,)), dma((8,)), dma((ROWS,)),
        ],
        compiler_params=pltpu.CompilerParams(
            collective_id=0, has_side_effects=True, vmem_limit_bytes=56 * 2**20
        ),
        cost_estimate=pl.CostEstimate(
            flops=2 * KALL * KALL * QW, bytes_accessed=12 * 2**20, transcendentals=0
        ),
    )(spectrum, group_courant.reshape(1, FREQS), coupling, wind_dir, sea_mask)


def solution(mesh):
    return jax.shard_map(
        body,
        mesh=mesh,
        in_specs=(
            P("comp", "band", None),
            P(),
            P("band", None),
            P("band", None),
            P("band", None),
            P(("band", "comp"), None),
            P(("band", "comp")),
        ),
        out_specs=P("comp", "band", None),
        check_vma=False,
    )
```

time: 101 us -> 81.3 us (0.80)
  the two profiles are of different devices: /device:TPU:1 before, /device:TPU:123 now
where the time goes in v2:
time: 81.3 us; the launch traced here: 81.2 us
  Pallas kernels  77.7 us (96%)
  local copies, waits for them, and re-layouts  3.42 us (4%)
    pallas_call x1, Pallas kernels, body(): pl.pallas_call(kernel, out_shape=jax.ShapeDtypeStruct((KD, ROWS, LON), F3...  77.7 us
    unnamed x1, local copies, waits for them, and re-layouts  3.42 us

profile of v2, /device:TPU:123, one launch (start us, length us, event | category | flops | bytes accessed | tf_op | source)
XLA Modules:
  0.0 81.2 jit_solution(12801288364880547305)
XLA Ops:
  0.0 77.7 %shard_map.55 = f32[108,4,1440]{2,1,0:T(4,128)} custom-call(f32[108,4,1440]{2,1,0:T(4,128)} %spec.1, f32[1,48]{1,0:T(1,128)} %bitcast.1, bf16[108,1728]{1,0:T(8,128)(2,1)} %coup.1, s32[4,1440]{1,0:T(4,128)} %wind.1, s32[4,1440]{1,0:T(4,128)} %sea.1), custom_call_target="tpu_custom_call" | custom-call | flops 2466250752 | bytes 12582912 | tf_op jit(solution)/shard_map/pallas_call | solution.py:466
  77.8 3.4 %copy.7 = f32[108,4,1440]{2,1,0:T(4,128)} copy(f32[108,4,1440]{2,1,0:T(4,128)} %shard_map.55) | data formatting | bytes 4976640

commit v3 on v2

--- a/solution.py
+++ b/solution.py
@@ -26,6 +26,21 @@
 step_time = 0.5
 wind_gain = 0.6
 damping = 0.4
+
+LAST = {1: 4, -1: 3}
+AT_START = [("start", 1, 1), ("start", -1, 1)]
+DURING = {
+    1: [("ring", 1, 1)],
+    2: [("ring", -1, 1)],
+    3: [("ring", 1, 2), ("xy", 1, 1), ("xy", -1, 1)],
+    5: [("ring", -1, 2), ("ring", 1, 3)],
+}
+BEFORE_S = [("xy", 1, 2), ("xy", -1, 2), ("ring", 1, 4), ("ring", -1, 3), ("xy", 1, 4), ("xy", 1, 3), ("xy", -1, 3)]
+AFTER_S = [("sib", 1, 1), ("sib", -1, 1), ("sib", 1, 2), ("sib", -1, 2),("sib", 1, 3), ("sib", -1, 3), ("sib", 1, 4)]
+NEAR = (0, 1, 2, 3, 4, 5, 6, 7)
+IN_NEAR = {}
+AFTER_NEAR = []
+FAR = ()
 
 MESH = pl.DeviceIdType.MESH
 F32 = jnp.float32
@@ -134,10 +149,12 @@
     mine = pl.ds(pl.multiple_of(half * HALF, 128), HALF)
     theirs = pl.ds(pl.multiple_of((1 - half) * HALF, 128), HALF)
 
-    def ring(block, step, n):
+    pieces = ((0, 64), (64, 48))
+
+    def ring(block, step, n, k):
+        part = C.at[block, pl.ds(*pieces[k]), mine]
         return pltpu.make_async_remote_copy(
-            src_ref=C.at[block, :, mine], dst_ref=C.at[block, :, mine],
-            send_sem=cs_sem, recv_sem=ring_sem.at[n],
+            src_ref=part, dst_ref=part, send_sem=cs_sem, recv_sem=ring_sem.at[n, k],
             device_id={"band": (b + step + 32) % 16}, device_id_type=MESH,
         )
 
@@ -148,23 +165,22 @@
         ((y + 3) % 4) * 4 + x,
     )
 
-    def spread(block, at):
-        for k, (lo, cnt) in enumerate(((0, 32), (32, 32), (64, 32), (96, 16))):
+    def spread(block, at, k):
+        for m, (lo, cnt) in enumerate((((0, 32), (32, 32)), ((64, 32), (96, 16)))[k]):
             piece = C.at[block, pl.ds(lo, cnt), mine]
             pltpu.make_async_remote_copy(
                 src_ref=piece, dst_ref=piece, send_sem=cs_sem, recv_sem=xy_sem.at[at],
-                device_id={"comp": xy[k]}, device_id_type=MESH,
+                device_id={"comp": xy[2 * k + m]}, device_id_type=MESH,
             ).start()
 
-    def to_sib(block, cols, n):
+    def to_sib(block, n, rows=pl.ds(0, KP), cols=pl.ds(0, KALL)):
+        part = C.at[block, rows, cols]
         return pltpu.make_async_remote_copy(
-            src_ref=C.at[block, :, cols], dst_ref=C.at[block, :, cols],
-            send_sem=cs_sem, recv_sem=sib_sem.at[n],
+            src_ref=part, dst_ref=part, send_sem=cs_sem, recv_sem=sib_sem.at[n],
             device_id={"band": sib}, device_id_type=MESH,
         )
 
-    events = ((1, 1), (-1, 1), (1, 2), (-1, 2), (1, 3), (-1, 3), (1, 4))
-    last = {1: 4, -1: 3}
+    events = [(1, s) for s in range(1, LAST[1] + 1)] + [(-1, s) for s in range(1, LAST[-1] + 1)]
 
     def block_of(side, s, base=None):
         base = b if base is None else base
@@ -173,27 +189,38 @@
     def distance(side, s):
         return (side * s * dirn + 8) % 8 - 1
 
-    def ring_event(n):
-        side, s = events[n]
+    def ring_start(side, s, block):
+        for k in range(2):
+            ring(block, -2 * side * dirn, events.index((side, s)), k).start()
+
+    def ring_event(side, s):
+        n = events.index((side, s))
         block = block_of(side, s)
-        ring(block, 0, n).wait_recv()
-        if s < last[side]:
-            ring(block, -2 * side * dirn, events.index((side, s + 1))).start()
-        spread(block, distance(side, s))
-        to_sib(block, mine, n).start()
-
-    def xy_event(n):
-        side, s = events[n]
+        for k in range(2):
+            ring(block, 0, n, k).wait_recv()
+            if s < LAST[side]:
+                ring(block, -2 * side * dirn, events.index((side, s + 1)), k).start()
+            spread(block, distance(side, s), k)
+            to_sib(block, n, pl.ds(*pieces[k]), mine).start()
+
+    def xy_event(side, s):
+        n = events.index((side, s))
         block = block_of(side, s)
         whole = C.at[block, :, theirs]
         pltpu.make_async_copy(whole, whole, xy_sem.at[distance(side, s)]).wait()
-        to_sib(block, theirs, n).start()
-
-    def sib_event(n):
-        side, s = events[n]
-        to_sib(block_of(side, s, sib), pl.ds(0, KALL), n).wait_recv()
-
-    ring(b, -2 * dirn, 0).start()
+        to_sib(block, n, cols=theirs).start()
+
+    def sib_event(side, s):
+        to_sib(block_of(side, s, sib), events.index((side, s))).wait_recv()
+
+    def run(steps):
+        for kind, side, s in steps:
+            if kind == "start":
+                ring_start(side, 1, b)
+            else:
+                {"ring": ring_event, "xy": xy_event, "sib": sib_event}[kind](side, s)
+
+    run(AT_START)
 
     @pl.when(has_send)
     def _():
@@ -214,8 +241,7 @@
         def _():
             halo(j).start()
 
-    ring(b, 2 * dirn, 1).start()
-    to_sib(b, pl.ds(0, KALL), 7).start()
+    to_sib(b, 7).start()
 
     shape = (KP, 128)
     comp = (row_iota(shape) + c * KD).astype(F32)
@@ -316,35 +342,17 @@
                 device_id={"comp": to}, device_id_type=MESH,
             ).start()
 
-        @pl.when(j == 2)
-        def _():
-            ring_event(0)
-
-        @pl.when(j == 3)
-        def _():
-            ring_event(1)
-
-        @pl.when(j == 4)
-        def _():
-            ring_event(2)
-            xy_event(0)
-            xy_event(1)
-
-        @pl.when(j == 5)
-        def _():
-            ring_event(3)
+        for at, steps in DURING.items():
+            @pl.when(j == at)
+            def _(steps=steps):
+                run(steps)
 
     S[pl.ds(pl.multiple_of(c * KP, CH), KP), :] = stage[c]
-    xy_event(2)
-    xy_event(3)
-    ring_event(4)
-    for n in (7, 0, 1, 2, 3):
-        if n == 7:
-            to_sib(sib, pl.ds(0, KALL), 7).wait_recv()
-        else:
-            sib_event(n)
+    run(BEFORE_S)
+    to_sib(sib, 7).wait_recv()
     rest = S.at[pl.ds(0, (NB - 1) * KP), :]
     pltpu.make_async_copy(rest, rest, sr_sem).wait()
+    run(AFTER_S)
 
     def back(to):
         return pltpu.make_async_remote_copy(
@@ -375,33 +383,27 @@
             def _():
                 back(to).start()
 
-    @pl.loop(0, 5)
+    def pick(group, n):
+        m = (n + c) % len(group)
+        away = group[0]
+        for k in range(1, len(group)):
+            away = jnp.where(m == k, group[k], away)
+        return (z + away) % 8
+
+    @pl.loop(0, len(NEAR))
     def _(n):
-        multiply((z + (n + c) % 5 + 6) % 8)
-
-        @pl.when(n == 0)
-        def _():
-            ring_event(5)
-
-        @pl.when(n == 1)
-        def _():
-            ring_event(6)
-
-        @pl.when(n == 2)
-        def _():
-            xy_event(4)
-            xy_event(5)
-
-        @pl.when(n == 3)
-        def _():
-            xy_event(6)
-
-    for n in (4, 5, 6):
-        sib_event(n)
-
-    @pl.loop(0, 3)
-    def _(n):
-        multiply((z + (n + c) % 3 + 3) % 8)
+        multiply(pick(NEAR, n))
+        for at, steps in IN_NEAR.items():
+            @pl.when(n == at)
+            def _(steps=steps):
+                run(steps)
+
+    run(AFTER_NEAR)
+    if FAR:
+
+        @pl.loop(0, len(FAR))
+        def _(n):
+            multiply(pick(FAR, n))
 
     trv[c] = tst[c]
 
@@ -485,7 +487,7 @@
             pltpu.VMEM((NB, KP, QW), jnp.int16),
             pltpu.VMEM((ROWS, 8, LP), F32),
             dma((NCH, ROWS)), dma, dma((NCH,)), dma, dma, dma, dma, dma, dma((NB,)),
-            dma, dma((7,)), dma((7,)), dma((8,)), dma((ROWS,)),
+            dma, dma((7, 2)), dma((7,)), dma((8,)), dma((ROWS,)),
         ],
         compiler_params=pltpu.CompilerParams(
             collective_id=0, has_side_effects=True, vmem_limit_bytes=56 * 2**20

time: 81.3 us -> 70.5 us (0.87)
  the two profiles are of different devices: /device:TPU:123 before, /device:TPU:1 now
where the time goes in v3:
time: 70.5 us; the launch traced here: 70.4 us
  Pallas kernels  67 us (95%)
  local copies, waits for them, and re-layouts  3.42 us (5%)
    pallas_call x1, Pallas kernels, body(): pl.pallas_call(kernel, out_shape=jax.ShapeDtypeStruct((KD, ROWS, LON), F3...  67 us
    unnamed x1, local copies, waits for them, and re-layouts  3.42 us

profile of v3, /device:TPU:1, one launch (start us, length us, event | category | flops | bytes accessed | tf_op | source)
XLA Modules:
  0.0 70.4 jit_solution(10253488126583840478)
XLA Ops:
  0.0 67.0 %shard_map.55 = f32[108,4,1440]{2,1,0:T(4,128)} custom-call(f32[108,4,1440]{2,1,0:T(4,128)} %spec.1, f32[1,48]{1,0:T(1,128)} %bitcast.1, bf16[108,1728]{1,0:T(8,128)(2,1)} %coup.1, s32[4,1440]{1,0:T(4,128)} %wind.1, s32[4,1440]{1,0:T(4,128)} %sea.1), custom_call_target="tpu_custom_call" | custom-call | flops 2466250752 | bytes 12582912 | tf_op jit(solution)/shard_map/pallas_call | solution.py:468
  67.0 3.4 %copy.7 = f32[108,4,1440]{2,1,0:T(4,128)} copy(f32[108,4,1440]{2,1,0:T(4,128)} %shard_map.55) | data formatting | bytes 4976640

commit v4 on v3

--- a/solution.py
+++ b/solution.py
@@ -29,18 +29,11 @@
 
 LAST = {1: 4, -1: 3}
 AT_START = [("start", 1, 1), ("start", -1, 1)]
-DURING = {
-    1: [("ring", 1, 1)],
-    2: [("ring", -1, 1)],
-    3: [("ring", 1, 2), ("xy", 1, 1), ("xy", -1, 1)],
-    5: [("ring", -1, 2), ("ring", 1, 3)],
-}
-BEFORE_S = [("xy", 1, 2), ("xy", -1, 2), ("ring", 1, 4), ("ring", -1, 3), ("xy", 1, 4), ("xy", 1, 3), ("xy", -1, 3)]
+DURING = {0: [("ring", 1, 1)], 2: [("ring", 1, 2), ("ring", -1, 1)], 4: [("ring", 1, 3), ("xy", 1, 1), ("xy", -1, 1)], 5: [("ring", -1, 2)], 6: [("ring", 1, 4)]}
+BEFORE_S = [("xy", 1, 2), ("xy", -1, 2), ("ring", -1, 3), ("xy", 1, 4), ("xy", 1, 3), ("xy", -1, 3)]
 AFTER_S = [("sib", 1, 1), ("sib", -1, 1), ("sib", 1, 2), ("sib", -1, 2),("sib", 1, 3), ("sib", -1, 3), ("sib", 1, 4)]
-NEAR = (0, 1, 2, 3, 4, 5, 6, 7)
-IN_NEAR = {}
-AFTER_NEAR = []
-FAR = ()
+
+ORDER = ((1, 0), (3, 1), (0, 1), (2, 0), (1, 1), (3, 0), (2, 1), (0, 0))
 
 MESH = pl.DeviceIdType.MESH
 F32 = jnp.float32
@@ -53,6 +46,22 @@
 
 def row_iota(shape):
     return lax.broadcasted_iota(jnp.int32, shape, 0)
+
+
+def sine(v):
+    square = v * v
+    total = jnp.full_like(v, 1.0 / math.factorial(13))
+    for n in (11, 9, 7, 5, 3, 1):
+        total = total * square + (-1.0) ** (n // 2) / math.factorial(n)
+    return total * v
+
+
+def cosine_of(step):
+    return sine((jnp.abs(step - 18.0) - 9.0) * (2.0 * math.pi / DIRS))
+
+
+def sine_of(step):
+    return cosine_of(jnp.where(step < 9.0, step + 27.0, step - 9.0))
 
 
 def kernel(
@@ -124,11 +133,7 @@
         return jnp.concatenate([v, v[:, :48], v[:, LON - 48 :]], axis=1)
 
     seas = wrap(sea[...].astype(F32))
-    angle = 2.0 * math.pi / DIRS * wind[...].astype(F32)
-    cosw, sinw = wrap(jnp.cos(angle)), wrap(jnp.sin(angle))
     for r in range(ROWS):
-        for k, v in enumerate((seas, cosw, sinw)):
-            aux[4 * k + row_of(r)] = jnp.broadcast_to(v[r : r + 1], (8, LP))
         mrow[row_of(r)] = seas[r : r + 1]
 
     pl.semaphore_wait(barrier, NB - 1 + 4)
@@ -137,6 +142,10 @@
         src_ref=mrow.at[pl.ds(2, 2)], dst_ref=mh, send_sem=ms_sem, recv_sem=mr_sem,
         device_id={"band": to_band}, device_id_type=MESH,
     )
+
+    @pl.when(has_send)
+    def _():
+        mask_copy.start()
 
     def halo(j):
         rows = rows_at(j)
@@ -221,10 +230,6 @@
                 {"ring": ring_event, "xy": xy_event, "sib": sib_event}[kind](side, s)
 
     run(AT_START)
-
-    @pl.when(has_send)
-    def _():
-        mask_copy.start()
 
     for j in range(NCH):
         count = CH if j < NCH - 1 else KD - CH * (NCH - 1)
@@ -243,6 +248,12 @@
 
     to_sib(b, 7).start()
 
+    blowing = wind[...].astype(F32)
+    cosw, sinw = wrap(cosine_of(blowing)), wrap(sine_of(blowing))
+    for r in range(ROWS):
+        for k, v in enumerate((seas, cosw, sinw)):
+            aux[4 * k + row_of(r)] = jnp.broadcast_to(v[r : r + 1], (8, LP))
+
     shape = (KP, 128)
     comp = (row_iota(shape) + c * KD).astype(F32)
     direction = jnp.floor((comp + 0.5) * (1.0 / FREQS))
@@ -250,20 +261,26 @@
     speeds = jnp.concatenate([gc[...], jnp.zeros((1, 128 - FREQS), F32)], axis=1)
     speed = jnp.sum(jnp.where(picked, speeds, 0.0), axis=1, keepdims=True)
     speed = jnp.where(row_iota(shape) < KD, speed, 0.0)
-    theta = 2.0 * math.pi / DIRS * direction
-    cosd, sind = jnp.cos(theta), jnp.sin(theta)
+    cosd, sind = cosine_of(direction), sine_of(direction)
     coef[8] = cosd
     coef[9] = sind
     coef[7] = jnp.abs(speed * sind)
     along = jnp.abs(speed * cosd)
     plane = row_iota((8, 128))
     row = (b * ROWS + jnp.where(up, plane - 3, 6 - plane)).astype(F32)
-    inverse = 1.0 / jnp.cos((first_lat + 0.25 * (row + 0.5)) * (math.pi / 180.0))
+    inverse = 1.0 / sine((90.0 - first_lat - 0.25 * (row + 0.5)) * (math.pi / 180.0))
     for p in range(7):
         coef[p] = along * inverse[p : p + 1]
 
     def wide(v, n):
         return jnp.concatenate([v] * n, axis=1)
+
+    def pair_of(n):
+        away, other = ORDER[0]
+        for k in range(1, len(ORDER)):
+            away = jnp.where(n == k, ORDER[k][0], away)
+            other = jnp.where(n == k, ORDER[k][1], other)
+        return ((y + jnp.where(core == 1, 4 - away, away)) % 4) * 2 + (x // 2 + other) % 2
 
     def advect(rows, shift):
         cols = [wide(coef[p, rows, :], LP // 128) for p in range(8)]
@@ -333,14 +350,18 @@
 
         place = pl.ds(pl.multiple_of(c * KP + j * CH, CH), CH)
 
-        @pl.loop(1, NB)
+        @pl.loop(0, len(ORDER))
         def _(n):
-            to = (c + n) % 16
-            pltpu.make_async_remote_copy(
-                src_ref=stage.at[to, rows, :], dst_ref=S.at[place, :],
-                send_sem=ss_sem, recv_sem=sr_sem,
-                device_id={"comp": to}, device_id_type=MESH,
-            ).start()
+            for k in range(2):
+                to = pair_of(n) * 2 + k
+
+                @pl.when(to != c)
+                def _():
+                    pltpu.make_async_remote_copy(
+                        src_ref=stage.at[to, rows, :], dst_ref=S.at[place, :],
+                        send_sem=ss_sem, recv_sem=sr_sem,
+                        device_id={"comp": to}, device_id_type=MESH,
+                    ).start()
 
         for at, steps in DURING.items():
             @pl.when(j == at)
@@ -383,27 +404,9 @@
             def _():
                 back(to).start()
 
-    def pick(group, n):
-        m = (n + c) % len(group)
-        away = group[0]
-        for k in range(1, len(group)):
-            away = jnp.where(m == k, group[k], away)
-        return (z + away) % 8
-
-    @pl.loop(0, len(NEAR))
+    @pl.loop(0, len(ORDER))
     def _(n):
-        multiply(pick(NEAR, n))
-        for at, steps in IN_NEAR.items():
-            @pl.when(n == at)
-            def _(steps=steps):
-                run(steps)
-
-    run(AFTER_NEAR)
-    if FAR:
-
-        @pl.loop(0, len(FAR))
-        def _(n):
-            multiply(pick(FAR, n))
+        multiply(pair_of(n))
 
     trv[c] = tst[c]
 
@@ -461,11 +464,26 @@
         result(i).wait()
 
 
+def hand_on(src, dst, held, sem, out_sem):
+    first, second = [], []
+    for k in range(4):
+        part = pl.ds(k * (KD // 4), KD // 4)
+        first.append(pltpu.make_async_copy(src.at[part], held.at[part], sem.at[k]))
+        second.append(pltpu.make_async_copy(held.at[part], dst.at[part], out_sem.at[k]))
+    for copy in first:
+        copy.start()
+    for k in range(4):
+        first[k].wait()
+        second[k].start()
+    for copy in second:
+        copy.wait()
+
+
 def body(spectrum, group_courant, coupling, wind_dir, sea_mask, owner_cells, owner_counts):
     vmem = pl.BlockSpec(memory_space=pltpu.VMEM)
     hbm = pl.BlockSpec(memory_space=pl.ANY)
     dma = pltpu.SemaphoreType.DMA
-    return pl.pallas_call(
+    staged = pl.pallas_call(
         kernel,
         out_shape=jax.ShapeDtypeStruct((KD, ROWS, LON), F32),
         in_specs=[hbm, vmem, vmem, vmem, vmem],
@@ -496,6 +514,13 @@
             flops=2 * KALL * KALL * QW, bytes_accessed=12 * 2**20, transcendentals=0
         ),
     )(spectrum, group_courant.reshape(1, FREQS), coupling, wind_dir, sea_mask)
+    return pl.pallas_call(
+        hand_on,
+        out_shape=jax.ShapeDtypeStruct((KD, ROWS, LON), F32),
+        in_specs=[hbm],
+        out_specs=hbm,
+        scratch_shapes=[pltpu.VMEM((KD, ROWS, LON), F32), dma((4,)), dma((4,))],
+    )(staged)
 
 
 def solution(mesh):

time: 70.5 us -> 66.7 us (0.946)
  local copies, waits for them, and re-layouts: 3.42 us -> 0 us
    unnamed x1 -> x0, local copies, waits for them, and re-layouts: 3.42 us -> none
    pallas_call x1, Pallas kernels: 67 us -> 64 us  [body(): pl.pallas_call(kernel, out_shape=jax.ShapeDtypeStruct((KD, ROWS, LON), F3...]
    pallas_call x0 -> x1, Pallas kernels: none -> 2.65 us  [body(): pl.pallas_call(hand_on, out_shape=jax.ShapeDtypeStruct((KD, ROWS, LON), F...]
where the time goes in v4:
time: 66.7 us; the launch traced here: 66.6 us
  Pallas kernels  66.6 us (100%)
    pallas_call x1, Pallas kernels, body(): pl.pallas_call(kernel, out_shape=jax.ShapeDtypeStruct((KD, ROWS, LON), F3...  64 us
    pallas_call x1, Pallas kernels, body(): pl.pallas_call(hand_on, out_shape=jax.ShapeDtypeStruct((KD, ROWS, LON), F...  2.65 us

profile of v4, /device:TPU:1, one launch (start us, length us, event | category | flops | bytes accessed | tf_op | source)
XLA Modules:
  0.0 66.6 jit_solution(8027006593990157257)
XLA Ops:
  0.0 64.0 %shard_map.55.src = f32[108,4,1440]{2,1,0:T(4,128)} custom-call(f32[108,4,1440]{2,1,0:T(4,128)} %spec.1, f32[1,48]{1,0:T(1,128)} %bitcast.1, bf16[108,1728]{1,0:T(8,128)(2,1)} %coup.1, s32[4,1440]{1,0:T(4,128)} %wind.1, s32[4,1440]{1,0:T(4,128)} %sea.1), custom_call_target="tpu_custom_call" | custom-call | flops 2466250752 | bytes 12582912 | tf_op jit(solution)/shard_map/pallas_call | solution.py:486
  64.0 2.7 %shard_map.56 = f32[108,4,1440]{2,1,0:T(4,128)} custom-call(f32[108,4,1440]{2,1,0:T(4,128)} %shard_map.55.src), custom_call_target="tpu_custom_call" | custom-call | tf_op jit(solution)/shard_map/pallas_call | solution.py:517

commit v5 on v4

--- a/solution.py
+++ b/solution.py
@@ -158,7 +158,7 @@
     mine = pl.ds(pl.multiple_of(half * HALF, 128), HALF)
     theirs = pl.ds(pl.multiple_of((1 - half) * HALF, 128), HALF)
 
-    pieces = ((0, 64), (64, 48))
+    pieces = ((0, 32), (32, 32), (64, 32), (96, 16))
 
     def ring(block, step, n, k):
         part = C.at[block, pl.ds(*pieces[k]), mine]
@@ -174,12 +174,16 @@
         ((y + 3) % 4) * 4 + x,
     )
 
+    def turned(way):
+        way = way % 4
+        return jnp.where(way == 0, xy[0], jnp.where(way == 1, xy[2], jnp.where(way == 2, xy[1], xy[3])))
+
     def spread(block, at, k):
-        for m, (lo, cnt) in enumerate((((0, 32), (32, 32)), ((64, 32), (96, 16)))[k]):
+        for m, (lo, cnt) in enumerate((pieces[k],)):
             piece = C.at[block, pl.ds(lo, cnt), mine]
             pltpu.make_async_remote_copy(
                 src_ref=piece, dst_ref=piece, send_sem=cs_sem, recv_sem=xy_sem.at[at],
-                device_id={"comp": xy[2 * k + m]}, device_id_type=MESH,
+                device_id={"comp": turned(k + at + core)}, device_id_type=MESH,
             ).start()
 
     def to_sib(block, n, rows=pl.ds(0, KP), cols=pl.ds(0, KALL)):
@@ -199,13 +203,13 @@
         return (side * s * dirn + 8) % 8 - 1
 
     def ring_start(side, s, block):
-        for k in range(2):
+        for k in range(4):
             ring(block, -2 * side * dirn, events.index((side, s)), k).start()
 
     def ring_event(side, s):
         n = events.index((side, s))
         block = block_of(side, s)
-        for k in range(2):
+        for k in range(4):
             ring(block, 0, n, k).wait_recv()
             if s < LAST[side]:
                 ring(block, -2 * side * dirn, events.index((side, s + 1)), k).start()
@@ -505,7 +509,7 @@
             pltpu.VMEM((NB, KP, QW), jnp.int16),
             pltpu.VMEM((ROWS, 8, LP), F32),
             dma((NCH, ROWS)), dma, dma((NCH,)), dma, dma, dma, dma, dma, dma((NB,)),
-            dma, dma((7, 2)), dma((7,)), dma((8,)), dma((ROWS,)),
+            dma, dma((7, 4)), dma((7,)), dma((8,)), dma((ROWS,)),
         ],
         compiler_params=pltpu.CompilerParams(
             collective_id=0, has_side_effects=True, vmem_limit_bytes=56 * 2**20

time: 66.7 us -> 66.7 us (level)
  no operation moved by 1% of the time
where the time goes in v5:
time: 66.7 us; the launch traced here: 66.6 us
  Pallas kernels  66.6 us (100%)
    pallas_call x1, Pallas kernels, body(): pl.pallas_call(kernel, out_shape=jax.ShapeDtypeStruct((KD, ROWS, LON), F3...  63.9 us
    pallas_call x1, Pallas kernels, body(): pl.pallas_call(hand_on, out_shape=jax.ShapeDtypeStruct((KD, ROWS, LON), F...  2.65 us

profile of v5, /device:TPU:1, one launch (start us, length us, event | category | flops | bytes accessed | tf_op | source)
XLA Modules:
  0.0 66.6 jit_solution(5940057119617513327)
XLA Ops:
  0.0 63.9 %shard_map.55.src = f32[108,4,1440]{2,1,0:T(4,128)} custom-call(f32[108,4,1440]{2,1,0:T(4,128)} %spec.1, f32[1,48]{1,0:T(1,128)} %bitcast.1, bf16[108,1728]{1,0:T(8,128)(2,1)} %coup.1, s32[4,1440]{1,0:T(4,128)} %wind.1, s32[4,1440]{1,0:T(4,128)} %sea.1), custom_call_target="tpu_custom_call" | custom-call | flops 2466250752 | bytes 12582912 | tf_op jit(solution)/shard_map/pallas_call | solution.py:490
  63.9 2.7 %shard_map.56 = f32[108,4,1440]{2,1,0:T(4,128)} custom-call(f32[108,4,1440]{2,1,0:T(4,128)} %shard_map.55.src), custom_call_target="tpu_custom_call" | custom-call | tf_op jit(solution)/shard_map/pallas_call | solution.py:521
